TPU v7x, 32 devices: a whole 2x2x4 slice. The times are simulated.
32 devices in a mesh: crop: 2 (over y), row: 16 (over z, x, core).
Axes of the slice: x: 2, y: 2, z: 4, core: 2. Of those that a mesh axis runs over, the one named last changes fastest.
Arguments:
- pair: bfloat16 [256, 128, 128], P(('crop', 'row')), parts along dimension 0, may hold values from -6 to 6
- residue_mask: int32 [256], P('crop'), parts along dimension 0, may hold values 0 or 1
- tri_proj: bfloat16 [2, 128, 512], replicated, may hold values from -0.5 to 0.5
- gate_out: bfloat16 [2, 128, 128], replicated, may hold values from -0.5 to 0.5
- w_out: bfloat16 [2, 128, 128], replicated, may hold values from -0.5 to 0.5
- norm_gain: float32 [2, 2, 128], replicated, may hold values from 0.25 to 1.75
Outputs:
- pair_out: bfloat16 [256, 128, 128], P(('crop', 'row')), parts along dimension 0
There are 2 independent parts, one for each index of `crop`. A program takes and returns all parts, laid end to end along the dimension named above; an argument that names none is the same for every part. Nothing has to cross between parts.
Inputs may be any that keep to these rules, and one draw needn't show every extreme that they name: `residue_mask`: 1 marks a valid residue, 0 a padded one.
All inputs are finite; a program needn't handle non-finite values.
Results may differ from a plain program's by a relative error of at most 0.012.
Values may be sent and summed in bfloat16 or wider, within the bound.
A program may use at most 64 MiB of HBM per device.

v0:
```python
import jax
import jax.numpy as jnp
from jax import lax
from jax.sharding import PartitionSpec as P


def layer_norm_lead(values, gain):
    centre = jnp.mean(values, axis=0, keepdims=True)
    spread = jnp.mean(jnp.square(values - centre), axis=0, keepdims=True)
    return (values - centre) * lax.rsqrt(spread + 1e-05) * gain[:, None, None]


def layer_norm_last(values, gain):
    centre = jnp.mean(values, axis=-1, keepdims=True)
    spread = jnp.mean(jnp.square(values - centre), axis=-1, keepdims=True)
    return (values - centre) * lax.rsqrt(spread + 1e-05) * gain


def tri_update(state, pair_mask, proj, gate_weight, out_weight, gain_in, gain_out, incoming):
    channels = state.shape[2]
    state_f = state.astype(jnp.float32)
    normed = layer_norm_last(state_f, gain_in).astype(jnp.bfloat16)
    projected = jnp.einsum("rnk,kc->crn", normed, proj, preferred_element_type=jnp.float32)
    left = (
        pair_mask * jax.nn.sigmoid(projected[channels : 2 * channels]) * projected[:channels]
    ).astype(jnp.bfloat16)
    right = (
        pair_mask
        * jax.nn.sigmoid(projected[3 * channels :])
        * projected[2 * channels : 3 * channels]
    ).astype(jnp.bfloat16)
    left_all = lax.all_to_all(left, "row", split_axis=0, concat_axis=1, tiled=True)
    right_all = lax.all_to_all(right, "row", split_axis=0, concat_axis=1, tiled=True)
    if incoming:
        product = jnp.einsum(
            "cki,ckj->cij", left_all, right_all, preferred_element_type=jnp.float32
        )
    else:
        product = jnp.einsum(
            "cik,cjk->cij", left_all, right_all, preferred_element_type=jnp.float32
        )
    returned = lax.all_to_all(
        product.astype(jnp.bfloat16), "row", split_axis=1, concat_axis=0, tiled=True
    )
    product_norm = layer_norm_lead(returned.astype(jnp.float32), gain_out).astype(jnp.bfloat16)
    gate_values = jax.nn.sigmoid(
        jnp.einsum("rnk,kd->rnd", normed, gate_weight, preferred_element_type=jnp.float32)
    )
    update = gate_values * jnp.einsum(
        "crn,cd->rnd", product_norm, out_weight, preferred_element_type=jnp.float32
    )
    return (state_f + update).astype(jnp.bfloat16)


def on_device(pair, residue_mask, tri_proj, gate_out, w_out, norm_gain):
    row_count = pair.shape[0]
    start = lax.axis_index("row") * row_count
    valid = residue_mask.astype(jnp.float32)
    row_valid = lax.dynamic_slice_in_dim(valid, start, row_count)
    pair_mask = row_valid[:, None] * valid[None, :]
    state = tri_update(
        pair, pair_mask, tri_proj[0], gate_out[0], w_out[0], norm_gain[0, 0], norm_gain[0, 1], False
    )
    state = tri_update(
        state, pair_mask, tri_proj[1], gate_out[1], w_out[1], norm_gain[1, 0], norm_gain[1, 1], True
    )
    return state


def solution(mesh):
    placed = (P(("crop", "row"), None, None), P("crop"), P(), P(), P(), P())
    return jax.shard_map(
        on_device,
        mesh=mesh,
        in_specs=placed,
        out_specs=P(("crop", "row"), None, None),
        check_vma=False,
    )
```

profile of v0, /device:TPU:0, one launch (start us, length us, event | category | flops | bytes accessed | tf_op | source)
XLA Modules:
  0.0 95.6 jit_solution(8113066999564752957)
XLA Ops:
  0.0 1.1 %copy.71 = bf16[8,128,128]{1,2,0:T(8,128)(2,1)S(1)} copy(bf16[8,128,128]{2,1,0:T(8,128)(2,1)} %param.6) | data formatting | bytes 524288 | tf_op args[0]
  1.2 0.1 fusion.13
  1.3 0.8 slice_bitcast_fusion
  2.1 0.7 convert_element_type.77
  2.7 0.1 dynamic_slice.3
  2.8 0.1 broadcast_multiply_fusion
  2.9 1.4 %convolution_bitcast_fusion.1 = f32[512,8,128]{0,2,1:T(8,128)S(1)} fusion(bf16[2,128,512]{2,1,0:T(8,128)(2,1)} %param.8, bf16[8,128,128]{1,2,0:T(8,128)(2,1)S(1)} %copy.71, f32[128]{0:T(128)S(1)} %get-tuple-element.12, f32[8,128]{1,0:T(8,128)S(1)} %add_rsqrt_fusion.3, f32[8,128]{1,0:T(8,128)S(1)} %broadcast_multiply_fusion.4), kind=kOutput, calls=%fused_computation.1 | convolution fusion | flops 134873088 | bytes 2499072 | tf_op jit(solution)/shard_map/rnk,kc->crn/dot_general | solution.py:23
  4.3 0.3 fusion.31
  4.6 0.0 copy-start.2
  4.6 0.9 copy.77
  5.5 7.4 %all-to-all-start.1 = ((bf16[128,8,128]{2,1,0:T(8,128)(2,1)}), bf16[128,8,128]{2,1,0:T(8,128)(2,1)S(1)}, u32[]{:S(2)}, u32[]{:S(2)}) async-start(bf16[128,8,128]{2,1,0:T(8,128)(2,1)} %copy.77), calls=%async_computation.1 | async-start | bytes 524288 | tf_op jit(solution)/shard_map/all_to_all | solution.py:33
  12.9 0.2 copy.75
  13.1 9.9 %all-to-all-done.1 = bf16[128,8,128]{2,1,0:T(8,128)(2,1)S(1)} async-done(((bf16[128,8,128]{2,1,0:T(8,128)(2,1)}), bf16[128,8,128]{2,1,0:T(8,128)(2,1)S(1)}, u32[]{:S(2)}, u32[]{:S(2)}) %all-to-all-start.1) | async-done | bytes 262176 | tf_op jit(solution)/shard_map/all_to_all | solution.py:33
  22.9 12.8 %all_to_all.90 = bf16[128,8,128]{2,1,0:T(8,128)(2,1)S(1)} all-to-all(bf16[128,8,128]{2,1,0:T(8,128)(2,1)S(1)} %copy.75), channel_id=1, replica_groups=mesh['crop'=2,'row'=16] {'row'}, dimensions={0} | all-to-all | bytes 524288 | tf_op jit(solution)/shard_map/all_to_all | solution.py:32
  35.7 0.3 convolution_convert_fusion.1
  36.0 0.0 copy-start.1
  36.1 0.9 copy.79
  36.9 3.5 %all-to-all-start.2 = ((bf16[8,128,128]{2,0,1:T(8,128)(2,1)}), bf16[8,128,128]{2,0,1:T(8,128)(2,1)S(1)}, u32[]{:S(2)}, u32[]{:S(2)}) async-start(bf16[8,128,128]{2,0,1:T(8,128)(2,1)} %copy.79), calls=%async_computation.2 | async-start | bytes 524288 | tf_op jit(solution)/shard_map/all_to_all | solution.py:42
  40.5 0.1 mul.156
  40.6 0.0 copy-done.2
  40.6 0.0 copy-start
  40.6 0.4 fusion.2
  40.9 9.5 %all-to-all-done.2 = bf16[8,128,128]{2,0,1:T(8,128)(2,1)S(1)} async-done(((bf16[8,128,128]{2,0,1:T(8,128)(2,1)}), bf16[8,128,128]{2,0,1:T(8,128)(2,1)S(1)}, u32[]{:S(2)}, u32[]{:S(2)}) %all-to-all-start.2) | async-done | bytes 262176 | tf_op jit(solution)/shard_map/all_to_all | solution.py:42
  50.5 0.1 fusion.44
  50.5 0.1 fusion.47
  50.6 0.0 copy-done.1
  50.7 0.3 fusion.75
  51.0 0.1 multiply_reduce_fusion
  51.1 0.5 convolution_bitcast_fusion
  51.6 0.3 fusion.21
  51.9 0.9 copy.85
  52.8 3.5 %all-to-all-start.3 = ((bf16[128,8,128]{2,1,0:T(8,128)(2,1)}), bf16[128,8,128]{2,1,0:T(8,128)(2,1)S(1)}, u32[]{:S(2)}, u32[]{:S(2)}) async-start(bf16[128,8,128]{2,1,0:T(8,128)(2,1)} %copy.85), calls=%async_computation.3 | async-start | bytes 524288 | tf_op jit(solution)/shard_map/all_to_all | solution.py:32
  56.3 0.2 copy.87
  56.5 9.8 %all-to-all-done.3 = bf16[128,8,128]{2,1,0:T(8,128)(2,1)S(1)} async-done(((bf16[128,8,128]{2,1,0:T(8,128)(2,1)}), bf16[128,8,128]{2,1,0:T(8,128)(2,1)S(1)}, u32[]{:S(2)}, u32[]{:S(2)}) %all-to-all-start.3) | async-done | bytes 262176 | tf_op jit(solution)/shard_map/all_to_all | solution.py:32
  66.4 12.8 %all_to_all.91 = bf16[128,8,128]{2,1,0:T(8,128)(2,1)S(1)} all-to-all(bf16[128,8,128]{2,1,0:T(8,128)(2,1)S(1)} %copy.87), channel_id=1, replica_groups=mesh['crop'=2,'row'=16] {'row'}, dimensions={0} | all-to-all | bytes 524288 | tf_op jit(solution)/shard_map/all_to_all | solution.py:33
  79.2 0.3 convolution_convert_fusion
  79.4 0.9 copy.90
  80.3 3.5 %all-to-all-start.5 = ((bf16[8,128,128]{2,0,1:T(8,128)(2,1)}), bf16[8,128,128]{2,0,1:T(8,128)(2,1)S(1)}, u32[]{:S(2)}, u32[]{:S(2)}) async-start(bf16[8,128,128]{2,0,1:T(8,128)(2,1)} %copy.90), calls=%async_computation.5 | async-start | bytes 524288 | tf_op jit(solution)/shard_map/all_to_all | solution.py:42
  83.9 0.1 mul.171
  84.0 0.1 copy.92
  84.0 0.4 fusion.5
  84.4 9.5 %all-to-all-done.5 = bf16[8,128,128]{2,0,1:T(8,128)(2,1)S(1)} async-done(((bf16[8,128,128]{2,0,1:T(8,128)(2,1)}), bf16[8,128,128]{2,0,1:T(8,128)(2,1)S(1)}, u32[]{:S(2)}, u32[]{:S(2)}) %all-to-all-start.5) | async-done | bytes 262176 | tf_op jit(solution)/shard_map/all_to_all | solution.py:42
  93.9 0.1 fusion.37
  94.0 0.1 fusion.40
  94.2 0.2 fusion.42
  94.4 0.1 copy.93
  94.4 0.3 fusion.10
  94.7 0.9 copy.96
  (10 shorter events, 0.1 us)
Async XLA Ops:
  4.6 35.9 %copy-start.2 = (bf16[2,128,128]{2,1,0:T(8,128)(2,1)S(1)}, bf16[2,128,128]{2,1,0:T(8,128)(2,1)}, u32[]{:S(2)}) copy-start(bf16[2,128,128]{2,1,0:T(8,128)(2,1)} %param.9) | copy-start | bytes 196612
  5.5 17.4 %all-to-all-start.1 = ((bf16[128,8,128]{2,1,0:T(8,128)(2,1)}), bf16[128,8,128]{2,1,0:T(8,128)(2,1)S(1)}, u32[]{:S(2)}, u32[]{:S(2)}) async-start(bf16[128,8,128]{2,1,0:T(8,128)(2,1)} %copy.77), calls=%async_computation.1 | async-start | bytes 524288 | tf_op jit(solution)/shard_map/all_to_all | solution.py:33
  36.0 14.6 %copy-start.1 = (bf16[2,128,128]{2,1,0:T(8,128)(2,1)S(1)}, bf16[2,128,128]{2,1,0:T(8,128)(2,1)}, u32[]{:S(2)}) copy-start(bf16[2,128,128]{2,1,0:T(8,128)(2,1)} %param.10) | copy-start | bytes 196612
  36.9 13.5 %all-to-all-start.2 = ((bf16[8,128,128]{2,0,1:T(8,128)(2,1)}), bf16[8,128,128]{2,0,1:T(8,128)(2,1)S(1)}, u32[]{:S(2)}, u32[]{:S(2)}) async-start(bf16[8,128,128]{2,0,1:T(8,128)(2,1)} %copy.79), calls=%async_computation.2 | async-start | bytes 524288 | tf_op jit(solution)/shard_map/all_to_all | solution.py:42
  40.6 10.5 %copy-start = (bf16[2,128,512]{2,1,0:T(8,128)(2,1)S(1)}, bf16[2,128,512]{2,1,0:T(8,128)(2,1)}, u32[]{:S(2)}) copy-start(bf16[2,128,512]{2,1,0:T(8,128)(2,1)} %param.8) | copy-start | bytes 786436
  52.8 13.5 %all-to-all-start.3 = ((bf16[128,8,128]{2,1,0:T(8,128)(2,1)}), bf16[128,8,128]{2,1,0:T(8,128)(2,1)S(1)}, u32[]{:S(2)}, u32[]{:S(2)}) async-start(bf16[128,8,128]{2,1,0:T(8,128)(2,1)} %copy.85), calls=%async_computation.3 | async-start | bytes 524288 | tf_op jit(solution)/shard_map/all_to_all | solution.py:32
  80.3 13.5 %all-to-all-start.5 = ((bf16[8,128,128]{2,0,1:T(8,128)(2,1)}), bf16[8,128,128]{2,0,1:T(8,128)(2,1)S(1)}, u32[]{:S(2)}, u32[]{:S(2)}) async-start(bf16[8,128,128]{2,0,1:T(8,128)(2,1)} %copy.90), calls=%async_computation.5 | async-start | bytes 524288 | tf_op jit(solution)/shard_map/all_to_all | solution.py:42
where the time goes:
time: 96.3 us; the launch traced here: 95.6 us
  waiting for transfers between devices  38.7 us (40%)
  blocking collectives  25.6 us (27%)
  starting transfers between devices  18 us (19%)
  local copies, waits for them, and re-layouts  7.03 us (7%)
  matrix products  3.83 us (4%)
  other arithmetic  2.22 us (2%)
    all_to_all x2, waiting for transfers between devices, tri_update(): lax.all_to_all(product.astype(jnp.bfloat16), 'row', split_axis=1, concat_...  19 us
    all_to_all x1, blocking collectives, tri_update(): lax.all_to_all(right, 'row', split_axis=0, concat_axis=1, tiled=True)  12.8 us
    all_to_all x1, blocking collectives, tri_update(): lax.all_to_all(left, 'row', split_axis=0, concat_axis=1, tiled=True)  12.8 us
    all_to_all x1, waiting for transfers between devices, tri_update(): lax.all_to_all(right, 'row', split_axis=0, concat_axis=1, tiled=True)  9.85 us
    all_to_all x1, waiting for transfers between devices, tri_update(): lax.all_to_all(left, 'row', split_axis=0, concat_axis=1, tiled=True)  9.81 us
    all_to_all x1, starting transfers between devices, tri_update(): lax.all_to_all(right, 'row', split_axis=0, concat_axis=1, tiled=True)  7.36 us
    all_to_all x2, starting transfers between devices, tri_update(): lax.all_to_all(product.astype(jnp.bfloat16), 'row', split_axis=1, concat_...  7.07 us
    all_to_all x1, starting transfers between devices, tri_update(): lax.all_to_all(left, 'row', split_axis=0, concat_axis=1, tiled=True)  3.53 us
  transfers between devices with their start and end apart: 4, of which 4 were waited for; matrix products, arithmetic and copies ran while one was open for 1% of the time, Pallas kernels for 0%

commit v1 on v0

v1 whole, which is shorter than its diff:
```python
import functools

import jax
import jax.numpy as jnp
from jax import lax
from jax.experimental import pallas as pl
from jax.experimental.pallas import tpu as pltpu
from jax.sharding import PartitionSpec as P

F32, BF16 = jnp.float32, jnp.bfloat16
LANES, SUBL = 128, 8


def layer_norm_lead(values, gain):
    centre = jnp.mean(values, axis=0, keepdims=True)
    spread = jnp.mean(jnp.square(values - centre), axis=0, keepdims=True)
    return (values - centre) * lax.rsqrt(spread + 1e-05) * gain[:, None, None]


def layer_norm_last(values, gain):
    centre = jnp.mean(values, axis=-1, keepdims=True)
    spread = jnp.mean(jnp.square(values - centre), axis=-1, keepdims=True)
    return (values - centre) * lax.rsqrt(spread + 1e-05) * gain


def tri_update(state, pair_mask, proj, gate_weight, out_weight, gain_in, gain_out, incoming):
    channels = state.shape[2]
    state_f = state.astype(F32)
    normed = layer_norm_last(state_f, gain_in).astype(BF16)
    projected = jnp.einsum("rnk,kc->crn", normed, proj, preferred_element_type=F32)
    left = (
        pair_mask * jax.nn.sigmoid(projected[channels : 2 * channels]) * projected[:channels]
    ).astype(BF16)
    right = (
        pair_mask
        * jax.nn.sigmoid(projected[3 * channels :])
        * projected[2 * channels : 3 * channels]
    ).astype(BF16)
    left_all = lax.all_to_all(left, "row", split_axis=0, concat_axis=1, tiled=True)
    right_all = lax.all_to_all(right, "row", split_axis=0, concat_axis=1, tiled=True)
    sums = "cki,ckj->cij" if incoming else "cik,cjk->cij"
    product = jnp.einsum(sums, left_all, right_all, preferred_element_type=F32)
    returned = lax.all_to_all(
        product.astype(BF16), "row", split_axis=1, concat_axis=0, tiled=True
    )
    product_norm = layer_norm_lead(returned.astype(F32), gain_out).astype(BF16)
    gate_values = jax.nn.sigmoid(
        jnp.einsum("rnk,kd->rnd", normed, gate_weight, preferred_element_type=F32)
    )
    update = gate_values * jnp.einsum(
        "crn,cd->rnd", product_norm, out_weight, preferred_element_type=F32
    )
    return (state_f + update).astype(BF16)


def general(pair, residue_mask, tri_proj, gate_out, w_out, norm_gain):
    row_count = pair.shape[0]
    start = lax.axis_index("row") * row_count
    valid = residue_mask.astype(F32)
    row_valid = lax.dynamic_slice_in_dim(valid, start, row_count)
    pair_mask = row_valid[:, None] * valid[None, :]
    state = pair
    for u in (0, 1):
        state = tri_update(
            state, pair_mask, tri_proj[u], gate_out[u], w_out[u],
            norm_gain[u, 0], norm_gain[u, 1], u == 1,
        )
    return state


def norm_lead(values, gain):
    centre = jnp.mean(values, axis=0, keepdims=True)
    moved = values - centre
    spread = jnp.mean(jnp.square(moved), axis=0, keepdims=True)
    return moved * lax.rsqrt(spread + 1e-05) * gain


def sigmoid(x):
    return 0.5 * jnp.tanh(0.5 * x) + 0.5


def far_first(ring):
    half = ring // 2
    order = [half]
    for step in range(1, half):
        order += [half - step, half + step]
    return order


def kernel(
    ring, rows,
    mask_s, mask_v, pair, proj, gate_w, out_w, gains,
    out,
    state, normed, gates, edge, prod,
    edge_send0, edge_send1, edge_recv0, edge_recv1,
    prod_send0, prod_send1, prod_recv0, prod_recv1,
    send_sem, recv_sem,
):
    me = lax.axis_index("row")
    chan = pair.shape[2]
    res = pair.shape[1]
    pairs = rows // 2
    order = far_first(ring)

    barrier = pltpu.get_barrier_semaphore()
    for o in order:
        pl.semaphore_signal(
            barrier, inc=1, device_id={"row": lax.rem(me + o, ring)},
            device_id_type=pl.DeviceIdType.MESH,
        )

    gains_t = gains[...].T
    valid = mask_v[...].astype(F32)

    def send(src, dst, o, phase):
        to = lax.rem(me + o, ring)
        pltpu.make_async_remote_copy(
            src_ref=src.at[to], dst_ref=dst.at[me],
            send_sem=send_sem.at[phase, to], recv_sem=recv_sem.at[phase, me],
            device_id={"row": to}, device_id_type=pl.DeviceIdType.MESH,
        ).start()

    def wait_recv(dst, o, phase):
        frm = lax.rem(me + o, ring)
        pltpu.make_async_remote_copy(
            src_ref=dst.at[frm], dst_ref=dst.at[frm],
            send_sem=send_sem.at[phase, frm], recv_sem=recv_sem.at[phase, frm],
            device_id={"row": frm}, device_id_type=pl.DeviceIdType.MESH,
        ).wait_recv()
        return frm

    def wait_send(src, o, phase):
        to = lax.rem(me + o, ring)
        pltpu.make_async_remote_copy(
            src_ref=src.at[to], dst_ref=src.at[to],
            send_sem=send_sem.at[phase, to], recv_sem=recv_sem.at[phase, to],
            device_id={"row": to}, device_id_type=pl.DeviceIdType.MESH,
        ).wait_send()

    def tiles(first, second):
        shape = (ring, SUBL, res)
        return jnp.concatenate([first.reshape(shape), second.reshape(shape)], axis=1)

    for p in range(pairs):
        for r in (0, 1):
            state[p, :, r * res : (r + 1) * res] = pair[2 * p + r].astype(F32).T

    for u in (0, 1):
        edge_send, edge_recv = ((edge_send0, edge_recv0), (edge_send1, edge_recv1))[u]
        prod_send, prod_recv = ((prod_send0, prod_recv0), (prod_send1, prod_recv1))[u]
        gain_in = gains_t[:, 2 * u : 2 * u + 1]
        gain_out = gains_t[:, 2 * u + 1 : 2 * u + 2]
        proj_t = proj[u].astype(F32).T.astype(BF16)

        for p in range(pairs):
            nb = norm_lead(state[p], gain_in).astype(BF16)
            normed[p] = nb
            projected = jnp.dot(proj_t, nb, preferred_element_type=F32)
            row_valid = [mask_s[me * rows + 2 * p + r].astype(F32) * valid for r in (0, 1)]
            both = jnp.concatenate(row_valid, axis=1)
            for side in (0, 1):
                at = 2 * side * chan
                value = projected[at : at + chan]
                gate = projected[at + chan : at + 2 * chan]
                block = value * sigmoid(gate) * both
                edge_send[:, side, p * 16 : (p + 1) * 16, :] = tiles(
                    block[:, :res], block[:, res:]
                ).astype(BF16)

        if u == 0:
            pl.semaphore_wait(barrier, ring - 1)
        for o in order:
            send(edge_send, edge_recv, o, 2 * u)

        gate_t = gate_w[u].astype(F32).T.astype(BF16)
        out_t = out_w[u].astype(F32).T.astype(BF16)
        for p in range(pairs):
            gates[p] = sigmoid(jnp.dot(gate_t, normed[p], preferred_element_type=F32))

        count = rows * SUBL
        for side in (0, 1):
            at = pl.multiple_of(me * count, count)
            edge[side, pl.ds(at, count), :] = edge_send[me, side].astype(F32)
        for o in reversed(order):
            frm = wait_recv(edge_recv, o, 2 * u)
            at = pl.multiple_of(frm * count, count)
            for side in (0, 1):
                edge[side, pl.ds(at, count), :] = edge_recv[frm, side].astype(F32)

        for c in range(SUBL):
            left = edge.at[0][pl.ds(c, res, stride=SUBL), :]
            right = edge.at[1][pl.ds(c, res, stride=SUBL), :].astype(BF16)
            if u == 1:
                product = jnp.dot(left.T.astype(BF16), right, preferred_element_type=F32)
            else:
                product = lax.dot_general(
                    left.astype(BF16), right, (((1,), (1,)), ((), ())),
                    preferred_element_type=F32,
                )
            prod[c * res : (c + 1) * res, :] = product

        def gather(to):
            for p in range(pairs):
                parts = [
                    prod[pl.ds(to * rows + 2 * p + r, SUBL, stride=res), :] for r in (0, 1)
                ]
                prod_send[to, p * 16 : (p + 1) * 16, :] = jnp.concatenate(
                    parts, axis=0
                ).astype(BF16)

        for o in order:
            gather(lax.rem(me + o, ring))
            send(prod_send, prod_recv, o, 2 * u + 1)
        gather(me)
        prod_recv[me] = prod_send[me]
        for o in reversed(order):
            wait_recv(prod_recv, o, 2 * u + 1)

        for p in range(pairs):
            got = prod_recv[:, p * 16 : (p + 1) * 16, :].astype(F32)
            for r in (0, 1):
                block = got[:, r * SUBL : (r + 1) * SUBL, :].reshape(chan, res)
                pn = norm_lead(block, gain_out).astype(BF16)
                lanes = slice(r * res, (r + 1) * res)
                update = jnp.dot(out_t, pn, preferred_element_type=F32)
                new = (state[p, :, lanes] + gates[p, :, lanes] * update).astype(BF16)
                if u == 0:
                    state[p, :, lanes] = new.astype(F32)
                else:
                    out[:, 2 * p + r, :] = new

    for u in (0, 1):
        for o in order:
            wait_send((edge_send0, edge_send1)[u], o, 2 * u)
            wait_send((prod_send0, prod_send1)[u], o, 2 * u + 1)


def fused(ring, pair, residue_mask, tri_proj, gate_out, w_out, norm_gain):
    rows, res, chan = pair.shape
    vmem = pl.BlockSpec(memory_space=pltpu.VMEM)
    count = rows * SUBL
    edges = pltpu.VMEM((ring, 2, count, res), BF16)
    products = pltpu.VMEM((ring, count, res), BF16)
    wide = (rows // 2, chan, 2 * res)
    out = pl.pallas_call(
        functools.partial(kernel, ring, rows),
        out_shape=jax.ShapeDtypeStruct((chan, rows, res), BF16),
        in_specs=[pl.BlockSpec(memory_space=pltpu.SMEM)] + [vmem] * 6,
        out_specs=vmem,
        scratch_shapes=[
            pltpu.VMEM(wide, F32),
            pltpu.VMEM(wide, BF16),
            pltpu.VMEM(wide, F32),
            pltpu.VMEM((2, ring * count, res), F32),
            pltpu.VMEM((SUBL * res, res), F32),
            edges, edges, edges, edges,
            products, products, products, products,
            pltpu.SemaphoreType.DMA((4, ring)),
            pltpu.SemaphoreType.DMA((4, ring)),
        ],
        compiler_params=pltpu.CompilerParams(
            collective_id=0, has_side_effects=True, vmem_limit_bytes=32 * 1024 * 1024
        ),
        name="triangle_updates",
    )(
        residue_mask, residue_mask.reshape(1, res), pair, tri_proj, gate_out, w_out,
        norm_gain.reshape(4, chan),
    )
    return jnp.moveaxis(out, 0, 2)


def on_device(ring, pair, *rest):
    rows, res, chan = pair.shape
    if chan == ring * SUBL and res == LANES and ring * rows == res and rows % 2 == 0:
        return fused(ring, pair, *rest)
    return general(pair, *rest)


def solution(mesh):
    placed = (P(("crop", "row"), None, None), P("crop"), P(), P(), P(), P())
    return jax.shard_map(
        functools.partial(on_device, mesh.shape["row"]),
        mesh=mesh,
        in_specs=placed,
        out_specs=P(("crop", "row"), None, None),
        check_vma=False,
    )
```

time: 96.3 us -> 55 us (0.57)
  Pallas kernels: 0 us -> 49.5 us
  waiting for transfers between devices: 38.7 us -> 0 us
  blocking collectives: 25.6 us -> 0 us
  starting transfers between devices: 18 us -> 0 us
  matrix products: 3.83 us -> 0 us
  other arithmetic: 2.22 us -> 0 us
  local copies, waits for them, and re-layouts: 7.03 us -> 5.16 us
    pallas_call x0 -> x1, Pallas kernels: none -> 49.5 us  [fused(): pl.pallas_call(functools.partial(kernel, ring, rows), out_shape=jax.Shape...]
    all_to_all x4 -> x0, waiting for transfers between devices: 38.7 us -> none  [the longest x2 19 us: tri_update(): lax.all_to_all(product.astype(jnp.bfloat16), 'row', split_axis=1, concat_...]
    all_to_all x2 -> x0, blocking collectives: 25.6 us -> none  [the longest x1 12.8 us: tri_update(): lax.all_to_all(right, 'row', split_axis=0, concat_axis=1, tiled=True)]
    all_to_all x4 -> x0, starting transfers between devices: 18 us -> none  [the longest x1 7.36 us: tri_update(): lax.all_to_all(right, 'row', split_axis=0, concat_axis=1, tiled=True)]
    convert_element_type x8 -> x0, local copies, waits for them, and re-layouts: 4.81 us -> none  [the longest x2 1.76 us: tri_update(): product.astype(jnp.bfloat16)]
    dot_general x8 -> x0, matrix products: 3.83 us -> none  [the longest x2 1.95 us: tri_update(): jnp.einsum('rnk,kc->crn', normed, proj, preferred_element_type=jnp.float32)]
    unnamed x7 -> x12, local copies, waits for them, and re-layouts: 1.14 us -> 4.26 us
    convert_element_type x4 -> x0, other arithmetic: 1.5 us -> none  [the longest x1 0.66 us: on_device(): valid = residue_mask.astype(jnp.float32)]
  transfers between devices with their start and end apart: 4 -> 0, of which waited for: 4 -> 0; matrix products, arithmetic and copies ran while one was open for 1% -> 0% of each run, Pallas kernels for 0% -> 0%
where the time goes in v1:
time: 55 us; the launch traced here: 54.7 us
  Pallas kernels  49.5 us (90%)
  local copies, waits for them, and re-layouts  5.16 us (9%)
    pallas_call x1, Pallas kernels, fused(): pl.pallas_call(functools.partial(kernel, ring, rows), out_shape=jax.Shape...  49.5 us
    unnamed x12, local copies, waits for them, and re-layouts  4.26 us

profile of v1, /device:TPU:0, one launch (start us, length us, event | category | flops | bytes accessed | tf_op | source)
XLA Modules:
  0.0 54.7 jit_solution(6433015777999912720)
XLA Ops:
  0.0 0.0 copy-start.4
  0.0 0.0 copy-start.5
  0.0 0.7 %copy-done.4 = f32[2,2,128]{2,1,0:T(2,128)S(1)} copy-done((f32[2,2,128]{2,1,0:T(2,128)S(1)}, f32[2,2,128]{2,1,0:T(2,128)}, u32[]{:S(2)}) %copy-start.4) | copy-done | bytes 2072
  0.7 0.0 copy-done.5
  0.7 0.0 copy-start
  0.7 0.9 %copy-done = bf16[8,128,128]{2,1,0:T(8,128)(2,1)S(1)} copy-done((bf16[8,128,128]{2,1,0:T(8,128)(2,1)S(1)}, bf16[8,128,128]{2,1,0:T(8,128)(2,1)}, u32[]{:S(2)}) %copy-start) | copy-done | bytes 262168
  1.6 0.0 copy-start.1
  1.6 0.9 %copy-done.1 = bf16[2,128,512]{2,1,0:T(8,128)(2,1)S(1)} copy-done((bf16[2,128,512]{2,1,0:T(8,128)(2,1)S(1)}, bf16[2,128,512]{2,1,0:T(8,128)(2,1)}, u32[]{:S(2)}) %copy-start.1) | copy-done | bytes 262168
  2.6 0.0 copy-start.2
  2.6 0.8 %copy-done.2 = bf16[2,128,128]{2,1,0:T(8,128)(2,1)S(1)} copy-done((bf16[2,128,128]{2,1,0:T(8,128)(2,1)S(1)}, bf16[2,128,128]{2,1,0:T(8,128)(2,1)}, u32[]{:S(2)}) %copy-start.2) | copy-done | bytes 65560
  3.4 0.0 copy-start.3
  3.4 0.8 %copy-done.3 = bf16[2,128,128]{2,1,0:T(8,128)(2,1)S(1)} copy-done((bf16[2,128,128]{2,1,0:T(8,128)(2,1)S(1)}, bf16[2,128,128]{2,1,0:T(8,128)(2,1)}, u32[]{:S(2)}) %copy-start.3) | copy-done | bytes 65560
  4.3 49.5 %triangle_updates.1 = bf16[128,8,128]{2,1,0:T(8,128)(2,1)S(1)} custom-call(s32[128]{0:T(128)S(1)} %copy-done.5, s32[1,128]{1,0:T(1,128)S(1)} %bitcast.5, bf16[8,128,128]{2,1,0:T(8,128)(2,1)S(1)} %copy-done, bf16[2,128,512]{2,1,0:T(8,128)(2,1)S(1)} %copy-done.1, bf16[2,128,128]{2,1,0:T(8,128)(2,1)S(1)} %copy-done.2, bf16[2,128,128]{2,1,0:T(8,128)(2,1)S(1)} %copy-done.3, ...), custom_call_target="tpu_custom_call" | custom-call | tf_op jit(solution)/shard_map/triangle_updates/pallas_call | solution.py:245
  53.8 0.9 %copy.7 = bf16[8,128,128]{2,1,0:T(8,128)(2,1)} copy(bf16[8,128,128]{1,0,2:T(8,128)(2,1)S(1)} %bitcast.3) | data formatting | bytes 524288 | tf_op jit(solution)/shard_map/transpose | solution.py:269
Async XLA Ops:
  0.0 0.7 %copy-start.4 = (f32[2,2,128]{2,1,0:T(2,128)S(1)}, f32[2,2,128]{2,1,0:T(2,128)}, u32[]{:S(2)}) copy-start(f32[2,2,128]{2,1,0:T(2,128)} %param.11) | copy-start | bytes 6148
  0.0 0.7 %copy-start.5 = (s32[128]{0:T(128)S(1)}, s32[128]{0:T(128)}, u32[]{:S(2)}) copy-start(s32[128]{0:T(128)} %mask_s.1) | copy-start | bytes 1540
  0.7 1.0 %copy-start = (bf16[8,128,128]{2,1,0:T(8,128)(2,1)S(1)}, bf16[8,128,128]{2,1,0:T(8,128)(2,1)}, u32[]{:S(2)}) copy-start(bf16[8,128,128]{2,1,0:T(8,128)(2,1)} %pair.1) | copy-start | bytes 786436
  1.6 0.9 %copy-start.1 = (bf16[2,128,512]{2,1,0:T(8,128)(2,1)S(1)}, bf16[2,128,512]{2,1,0:T(8,128)(2,1)}, u32[]{:S(2)}) copy-start(bf16[2,128,512]{2,1,0:T(8,128)(2,1)} %proj.1) | copy-start | bytes 786436
  2.6 0.8 %copy-start.2 = (bf16[2,128,128]{2,1,0:T(8,128)(2,1)S(1)}, bf16[2,128,128]{2,1,0:T(8,128)(2,1)}, u32[]{:S(2)}) copy-start(bf16[2,128,128]{2,1,0:T(8,128)(2,1)} %gate_w.1) | copy-start | bytes 196612
  3.4 0.8 %copy-start.3 = (bf16[2,128,128]{2,1,0:T(8,128)(2,1)S(1)}, bf16[2,128,128]{2,1,0:T(8,128)(2,1)}, u32[]{:S(2)}) copy-start(bf16[2,128,128]{2,1,0:T(8,128)(2,1)} %out_w.1) | copy-start | bytes 196612

commit v2 on v0

v2 whole, which is shorter than its diff:
```python
import functools

import jax
import jax.numpy as jnp
from jax import lax
from jax.experimental import pallas as pl
from jax.experimental.pallas import tpu as pltpu
from jax.sharding import PartitionSpec as P

F32, BF16 = jnp.float32, jnp.bfloat16
LANES, SUBL = 128, 8


def layer_norm_lead(values, gain):
    centre = jnp.mean(values, axis=0, keepdims=True)
    spread = jnp.mean(jnp.square(values - centre), axis=0, keepdims=True)
    return (values - centre) * lax.rsqrt(spread + 1e-05) * gain[:, None, None]


def layer_norm_last(values, gain):
    centre = jnp.mean(values, axis=-1, keepdims=True)
    spread = jnp.mean(jnp.square(values - centre), axis=-1, keepdims=True)
    return (values - centre) * lax.rsqrt(spread + 1e-05) * gain


def tri_update(state, pair_mask, proj, gate_weight, out_weight, gain_in, gain_out, incoming):
    channels = state.shape[2]
    state_f = state.astype(F32)
    normed = layer_norm_last(state_f, gain_in).astype(BF16)
    projected = jnp.einsum("rnk,kc->crn", normed, proj, preferred_element_type=F32)
    left = (
        pair_mask * jax.nn.sigmoid(projected[channels : 2 * channels]) * projected[:channels]
    ).astype(BF16)
    right = (
        pair_mask
        * jax.nn.sigmoid(projected[3 * channels :])
        * projected[2 * channels : 3 * channels]
    ).astype(BF16)
    left_all = lax.all_to_all(left, "row", split_axis=0, concat_axis=1, tiled=True)
    right_all = lax.all_to_all(right, "row", split_axis=0, concat_axis=1, tiled=True)
    sums = "cki,ckj->cij" if incoming else "cik,cjk->cij"
    product = jnp.einsum(sums, left_all, right_all, preferred_element_type=F32)
    returned = lax.all_to_all(
        product.astype(BF16), "row", split_axis=1, concat_axis=0, tiled=True
    )
    product_norm = layer_norm_lead(returned.astype(F32), gain_out).astype(BF16)
    gate_values = jax.nn.sigmoid(
        jnp.einsum("rnk,kd->rnd", normed, gate_weight, preferred_element_type=F32)
    )
    update = gate_values * jnp.einsum(
        "crn,cd->rnd", product_norm, out_weight, preferred_element_type=F32
    )
    return (state_f + update).astype(BF16)


def general(pair, residue_mask, tri_proj, gate_out, w_out, norm_gain):
    row_count = pair.shape[0]
    start = lax.axis_index("row") * row_count
    valid = residue_mask.astype(F32)
    row_valid = lax.dynamic_slice_in_dim(valid, start, row_count)
    pair_mask = row_valid[:, None] * valid[None, :]
    state = pair
    for u in (0, 1):
        state = tri_update(
            state, pair_mask, tri_proj[u], gate_out[u], w_out[u],
            norm_gain[u, 0], norm_gain[u, 1], u == 1,
        )
    return state


def norm_lead(values, gain):
    centre = jnp.mean(values, axis=0, keepdims=True)
    moved = values - centre
    spread = jnp.mean(jnp.square(moved), axis=0, keepdims=True)
    return moved * lax.rsqrt(spread + 1e-05) * gain


def sigmoid(x):
    return 0.5 * jnp.tanh(0.5 * x) + 0.5


def far_first(ring):
    half = ring // 2
    order = [half]
    for step in range(1, half):
        order += [half - step, half + step]
    return order


CHUNKS = 2
RIGHT, LEFT, BACK, EDGE, DONE = range(5)


def kernel(
    ring, rows,
    mask_h, pair_h, proj_h, gate_h, out_h, gains_h,
    out,
    mask_v, pair, proj, gate_w, out_w, gains,
    state, normed, gates,
    right_f, left_f, right_b, prod0, edge_f, prod1,
    right_send, right_recv, left_send, left_recv, back_send, back_recv,
    edge_send, edge_recv, done_send, done_recv,
    load_sem, send_sem, recv_sem,
):
    me = lax.axis_index("row")
    chan = pair.shape[2]
    res = pair.shape[1]
    half = ring // 2
    group = chan // half
    place = lax.rem(me, half)
    base = me - place
    per = rows // CHUNKS
    duos = per // 2
    everyone = far_first(ring)
    nearby = far_first(half)

    loads = [
        pltpu.make_async_copy(src, dst, load_sem.at[at])
        for at, (src, dst) in enumerate(
            ((pair_h, pair), (gains_h, gains), (proj_h, proj), (mask_h, mask_v),
             (gate_h, gate_w), (out_h, out_w))
        )
    ]
    for load in loads:
        load.start()

    barrier = pltpu.get_barrier_semaphore()
    for o in everyone:
        pl.semaphore_signal(
            barrier, inc=1, device_id={"row": lax.rem(me + o, ring)},
            device_id_type=pl.DeviceIdType.MESH,
        )

    def copy(src, dst, to, kind, ch, frm):
        return pltpu.make_async_remote_copy(
            src_ref=src, dst_ref=dst,
            send_sem=send_sem.at[kind, ch, to], recv_sem=recv_sem.at[kind, ch, frm],
            device_id={"row": to}, device_id_type=pl.DeviceIdType.MESH,
        )

    def far(o):
        return lax.rem(me + o, ring)

    def near(o):
        return base + lax.rem(place + o, half)

    def slot(device):
        return lax.rem(device, half)

    span = per * group

    def part(ch):
        return pl.ds(ch * span, span)

    loads[0].wait()
    loads[1].wait()
    gains_t = gains[...].T
    for r in range(rows):
        state[r] = pair[r].astype(F32).T

    def norm_rows(ch, gain):
        for r in range(ch * per, (ch + 1) * per):
            lanes = slice((r - ch * per) * res, (r - ch * per + 1) * res)
            normed[ch, :, lanes] = norm_lead(state[r], gain).astype(BF16)

    def edges(ch, weights_t):
        both = jnp.dot(weights_t, normed[ch], preferred_element_type=F32)
        return both[:chan] * sigmoid(both[chan:])

    norm_rows(0, gains_t[:, 0:1])
    loads[2].wait()
    loads[3].wait()
    valid = mask_v[...].astype(F32)
    lane = lax.broadcasted_iota(jnp.int32, (rows, res), 1)
    own = lax.broadcasted_iota(jnp.int32, (rows, res), 0) + me * rows
    own_valid = jnp.sum(
        jnp.where(lane == own, jnp.broadcast_to(valid, (rows, res)), 0.0), axis=1, keepdims=True
    )
    pair_mask = own_valid * valid

    def masked(ch, block):
        return [
            block[:, k * res : (k + 1) * res] * pair_mask[ch * per + k : ch * per + k + 1, :]
            for k in range(per)
        ]

    proj_t = proj[0].astype(F32).T.astype(BF16)
    for side, buf in ((1, right_send), (0, left_send)):
        for ch in range(CHUNKS):
            if side == 1 and ch > 0:
                norm_rows(ch, gains_t[:, 0:1])
            block = masked(ch, edges(ch, proj_t[2 * side * chan : 2 * (side + 1) * chan]))
            for k in range(per):
                at = (ch * per + k) * group
                buf[:, at : at + group, :] = block[k].reshape(half, group, res).astype(BF16)
            if side == 1:
                if ch == 0:
                    pl.semaphore_wait(barrier, ring - 1)
                for o in everyone:
                    to = far(o)
                    copy(
                        right_send.at[slot(to), part(ch)], right_recv.at[me, part(ch)],
                        to, RIGHT, ch, me,
                    ).start()
            else:
                for o in nearby:
                    to = near(o)
                    copy(
                        left_send.at[slot(to), part(ch)], left_recv.at[place, part(ch)],
                        to, LEFT, ch, me,
                    ).start()

    loads[4].wait()
    loads[5].wait()
    gate_t = [gate_w[u].astype(F32).T.astype(BF16) for u in (0, 1)]
    out_t = [out_w[u].astype(F32).T.astype(BF16) for u in (0, 1)]
    for ch in range(CHUNKS):
        gates[ch] = sigmoid(jnp.dot(gate_t[0], normed[ch], preferred_element_type=F32))

    def hold_right(device, ch, values):
        at = pl.multiple_of(device * (rows * group) + ch * span, span)
        right_f[pl.ds(at, span), :] = values.astype(F32)

    def hold_left(where, ch, values):
        at = pl.multiple_of(ch * (half * span) + where * span, span)
        left_f[pl.ds(at, span), :] = values.astype(F32)

    for ch in range(CHUNKS):
        hold_right(me, ch, right_send[place, part(ch), :])
        hold_left(place, ch, left_send[place, part(ch), :])
    for ch in range(CHUNKS):
        for o in reversed(everyone):
            frm = far(o)
            landed = right_recv.at[frm, part(ch)]
            copy(landed, landed, frm, RIGHT, ch, frm).wait_recv()
            hold_right(frm, ch, right_recv[frm, part(ch), :])
    for c in range(group):
        right_b[c] = right_f[pl.ds(c, res, stride=group), :].astype(BF16)
    count = half * per
    for ch in range(CHUNKS):
        for o in reversed(nearby):
            frm = near(o)
            landed = left_recv.at[slot(frm), part(ch)]
            copy(landed, landed, frm, LEFT, ch, frm).wait_recv()
            hold_left(slot(frm), ch, left_recv[slot(frm), part(ch), :])
        for c in range(group):
            left = left_f[pl.ds(ch * half * span + c, count, stride=group), :].astype(BF16)
            prod0[ch, c * count : (c + 1) * count, :] = lax.dot_general(
                left, right_b[c], (((1,), (1,)), ((), ())), preferred_element_type=F32
            )

        def give(where):
            for k in range(per):
                at = (ch * per + k) * group
                rows_of = prod0.at[ch][pl.ds(where * per + k, group, stride=count), :]
                back_send[where, at : at + group, :] = rows_of.astype(BF16)

        for o in nearby:
            to = near(o)
            give(slot(to))
            copy(
                back_send.at[slot(to), part(ch)], back_recv.at[place, part(ch)],
                to, BACK, ch, me,
            ).start()
        give(place)
        back_recv[place, part(ch), :] = back_send[place, part(ch), :]

    proj_t = proj[1].astype(F32).T.astype(BF16)
    size = per * SUBL
    for ch in range(CHUNKS):
        for o in reversed(nearby):
            frm = near(o)
            landed = back_recv.at[slot(frm), part(ch)]
            copy(landed, landed, frm, BACK, ch, frm).wait_recv()
        for k in range(per):
            r = ch * per + k
            got = back_recv[:, r * group : (r + 1) * group, :].reshape(chan, res)
            pn = norm_lead(got.astype(F32), gains_t[:, 1:2]).astype(BF16)
            update = jnp.dot(out_t[0], pn, preferred_element_type=F32)
            new = state[r] + gates[ch, :, k * res : (k + 1) * res] * update
            state[r] = new.astype(BF16).astype(F32)
        norm_rows(ch, gains_t[:, 2:3])
        for side in (0, 1):
            block = masked(ch, edges(ch, proj_t[2 * side * chan : 2 * (side + 1) * chan]))
            for d in range(duos):
                shape = (ring, SUBL, res)
                at = side * size + d * 16
                edge_send[ch, :, at : at + 16, :] = jnp.concatenate(
                    [block[2 * d].reshape(shape), block[2 * d + 1].reshape(shape)], axis=1
                ).astype(BF16)
        for o in everyone:
            to = far(o)
            copy(edge_send.at[ch, to], edge_recv.at[ch, me], to, EDGE, ch, me).start()

    for ch in range(CHUNKS):
        gates[ch] = sigmoid(jnp.dot(gate_t[1], normed[ch], preferred_element_type=F32))

    def hold_edges(device, ch, values):
        at = pl.multiple_of((ch * ring + device) * size, size)
        for side in (0, 1):
            edge_f[side, pl.ds(at, size), :] = values[side * size : (side + 1) * size].astype(F32)

    for ch in range(CHUNKS):
        hold_edges(me, ch, edge_send[ch, me])
        for o in reversed(everyone):
            frm = far(o)
            landed = edge_recv.at[ch, frm]
            copy(landed, landed, frm, EDGE, ch, frm).wait_recv()
            hold_edges(frm, ch, edge_recv[ch, frm])
    for c in range(SUBL):
        left = edge_f.at[0][pl.ds(c, res, stride=SUBL), :].T.astype(BF16)
        right = edge_f.at[1][pl.ds(c, res, stride=SUBL), :].astype(BF16)
        prod1[c * res : (c + 1) * res, :] = jnp.dot(left, right, preferred_element_type=F32)
    for ch in range(CHUNKS):

        def give_back(to):
            for d in range(duos):
                at = to * rows + ch * per + 2 * d
                parts = [prod1[pl.ds(at + k, SUBL, stride=res), :] for k in (0, 1)]
                done_send[ch, to, d * 16 : (d + 1) * 16, :] = jnp.concatenate(
                    parts, axis=0
                ).astype(BF16)

        for o in everyone:
            to = far(o)
            give_back(to)
            copy(done_send.at[ch, to], done_recv.at[ch, me], to, DONE, ch, me).start()
        give_back(me)
        done_recv[ch, me] = done_send[ch, me]

    for ch in range(CHUNKS):
        for o in reversed(everyone):
            frm = far(o)
            landed = done_recv.at[ch, frm]
            copy(landed, landed, frm, DONE, ch, frm).wait_recv()
        for d in range(duos):
            got = done_recv[ch, :, d * 16 : (d + 1) * 16, :].astype(F32)
            for j in (0, 1):
                k = 2 * d + j
                r = ch * per + k
                block = got[:, j * SUBL : (j + 1) * SUBL, :].reshape(chan, res)
                pn = norm_lead(block, gains_t[:, 3:4]).astype(BF16)
                update = jnp.dot(out_t[1], pn, preferred_element_type=F32)
                new = state[r] + gates[ch, :, k * res : (k + 1) * res] * update
                out[:, r, :] = new.astype(BF16)

    for ch in range(CHUNKS):
        for o in everyone:
            to = far(o)
            for kind, src in (
                (RIGHT, right_send.at[slot(to), part(ch)]),
                (EDGE, edge_send.at[ch, to]),
                (DONE, done_send.at[ch, to]),
            ):
                copy(src, src, to, kind, ch, to).wait_send()
        for o in nearby:
            to = near(o)
            for kind, src in (
                (LEFT, left_send.at[slot(to), part(ch)]),
                (BACK, back_send.at[slot(to), part(ch)]),
            ):
                copy(src, src, to, kind, ch, to).wait_send()


def fused(ring, pair, residue_mask, tri_proj, gate_out, w_out, norm_gain):
    rows, res, chan = pair.shape
    half = ring // 2
    group = chan // half
    per = rows // CHUNKS
    wide = (CHUNKS, chan, per * res)
    right_all = pltpu.VMEM((ring, rows * group, res), BF16)
    near_all = pltpu.VMEM((half, rows * group, res), BF16)
    edge_all = pltpu.VMEM((CHUNKS, ring, 2 * per * SUBL, res), BF16)
    done_all = pltpu.VMEM((CHUNKS, ring, per * SUBL, res), BF16)
    operands = (
        residue_mask.reshape(1, res), pair, tri_proj, gate_out, w_out, norm_gain.reshape(4, chan),
    )
    out = pl.pallas_call(
        functools.partial(kernel, ring, rows),
        out_shape=jax.ShapeDtypeStruct((chan, rows, res), BF16),
        in_specs=[pl.BlockSpec(memory_space=pl.ANY)] * 6,
        out_specs=pl.BlockSpec(memory_space=pltpu.VMEM),
        scratch_shapes=[pltpu.VMEM(x.shape, x.dtype) for x in operands]
        + [
            pltpu.VMEM((rows, chan, res), F32),
            pltpu.VMEM(wide, BF16),
            pltpu.VMEM(wide, F32),
            pltpu.VMEM((ring * rows * group, res), F32),
            pltpu.VMEM((half * rows * group, res), F32),
            pltpu.VMEM((group, res, res), BF16),
            pltpu.VMEM((CHUNKS, group * half * per, res), F32),
            pltpu.VMEM((2, ring * rows * SUBL, res), F32),
            pltpu.VMEM((SUBL * res, res), F32),
            near_all, right_all, near_all, near_all, near_all, near_all,
            edge_all, edge_all, done_all, done_all,
            pltpu.SemaphoreType.DMA((6,)),
            pltpu.SemaphoreType.DMA((5, CHUNKS, ring)),
            pltpu.SemaphoreType.DMA((5, CHUNKS, ring)),
        ],
        compiler_params=pltpu.CompilerParams(
            collective_id=0, has_side_effects=True, vmem_limit_bytes=40 * 1024 * 1024
        ),
        name="triangle_updates",
    )(*operands)
    return jnp.moveaxis(out, 0, 2)


def on_device(ring, pair, *rest):
    rows, res, chan = pair.shape
    fits = chan == ring * SUBL and res == LANES and ring * rows == res
    if fits and rows % (2 * CHUNKS) == 0 and ring % 2 == 0:
        return fused(ring, pair, *rest)
    return general(pair, *rest)


def solution(mesh):
    placed = (P(("crop", "row"), None, None), P("crop"), P(), P(), P(), P())
    return jax.shard_map(
        functools.partial(on_device, mesh.shape["row"]),
        mesh=mesh,
        in_specs=placed,
        out_specs=P(("crop", "row"), None, None),
        check_vma=False,
    )
```

time: 96.3 us -> 55.1 us (0.57)
  Pallas kernels: 0 us -> 49.7 us
  waiting for transfers between devices: 38.7 us -> 0 us
  blocking collectives: 25.6 us -> 0 us
  starting transfers between devices: 18 us -> 0 us
  matrix products: 3.83 us -> 0 us
  other arithmetic: 2.22 us -> 0 us
  local copies, waits for them, and re-layouts: 7.03 us -> 5.16 us
    pallas_call x0 -> x1, Pallas kernels: none -> 49.7 us  [fused(): pl.pallas_call(functools.partial(kernel, ring, rows), out_shape=jax.Shape...]
    all_to_all x4 -> x0, waiting for transfers between devices: 38.7 us -> none  [the longest x2 19 us: tri_update(): lax.all_to_all(product.astype(jnp.bfloat16), 'row', split_axis=1, concat_...]
    all_to_all x2 -> x0, blocking collectives: 25.6 us -> none  [the longest x1 12.8 us: tri_update(): lax.all_to_all(right, 'row', split_axis=0, concat_axis=1, tiled=True)]
    all_to_all x4 -> x0, starting transfers between devices: 18 us -> none  [the longest x1 7.36 us: tri_update(): lax.all_to_all(right, 'row', split_axis=0, concat_axis=1, tiled=True)]
    convert_element_type x8 -> x0, local copies, waits for them, and re-layouts: 4.81 us -> none  [the longest x2 1.76 us: tri_update(): product.astype(jnp.bfloat16)]
    dot_general x8 -> x0, matrix products: 3.83 us -> none  [the longest x2 1.95 us: tri_update(): jnp.einsum('rnk,kc->crn', normed, proj, preferred_element_type=jnp.float32)]
    unnamed x7 -> x12, local copies, waits for them, and re-layouts: 1.14 us -> 4.26 us
    convert_element_type x4 -> x0, other arithmetic: 1.5 us -> none  [the longest x1 0.66 us: on_device(): valid = residue_mask.astype(jnp.float32)]
  transfers between devices with their start and end apart: 4 -> 0, of which waited for: 4 -> 0; matrix products, arithmetic and copies ran while one was open for 1% -> 0% of each run, Pallas kernels for 0% -> 0%
where the time goes in v2:
time: 55.1 us; the launch traced here: 54.9 us
  Pallas kernels  49.7 us (90%)
  local copies, waits for them, and re-layouts  5.16 us (9%)
    pallas_call x1, Pallas kernels, fused(): pl.pallas_call(functools.partial(kernel, ring, rows), out_shape=jax.Shape...  49.7 us
    unnamed x12, local copies, waits for them, and re-layouts  4.26 us

profile of v2, /device:TPU:0, one launch (start us, length us, event | category | flops | bytes accessed | tf_op | source)
XLA Modules:
  0.0 54.9 jit_solution(940737720839407943)
XLA Ops:
  0.0 0.0 copy-start.4
  0.0 0.0 copy-start.5
  0.0 0.7 %copy-done.4 = f32[2,2,128]{2,1,0:T(2,128)S(1)} copy-done((f32[2,2,128]{2,1,0:T(2,128)S(1)}, f32[2,2,128]{2,1,0:T(2,128)}, u32[]{:S(2)}) %copy-start.4) | copy-done | bytes 2072
  0.7 0.0 copy-done.5
  0.7 0.0 copy-start
  0.7 0.9 %copy-done = bf16[8,128,128]{2,1,0:T(8,128)(2,1)S(1)} copy-done((bf16[8,128,128]{2,1,0:T(8,128)(2,1)S(1)}, bf16[8,128,128]{2,1,0:T(8,128)(2,1)}, u32[]{:S(2)}) %copy-start) | copy-done | bytes 262168
  1.6 0.0 copy-start.1
  1.6 0.9 %copy-done.1 = bf16[2,128,512]{2,1,0:T(8,128)(2,1)S(1)} copy-done((bf16[2,128,512]{2,1,0:T(8,128)(2,1)S(1)}, bf16[2,128,512]{2,1,0:T(8,128)(2,1)}, u32[]{:S(2)}) %copy-start.1) | copy-done | bytes 262168
  2.6 0.0 copy-start.2
  2.6 0.8 %copy-done.2 = bf16[2,128,128]{2,1,0:T(8,128)(2,1)S(1)} copy-done((bf16[2,128,128]{2,1,0:T(8,128)(2,1)S(1)}, bf16[2,128,128]{2,1,0:T(8,128)(2,1)}, u32[]{:S(2)}) %copy-start.2) | copy-done | bytes 65560
  3.4 0.0 copy-start.3
  3.4 0.8 %copy-done.3 = bf16[2,128,128]{2,1,0:T(8,128)(2,1)S(1)} copy-done((bf16[2,128,128]{2,1,0:T(8,128)(2,1)S(1)}, bf16[2,128,128]{2,1,0:T(8,128)(2,1)}, u32[]{:S(2)}) %copy-start.3) | copy-done | bytes 65560
  4.3 49.7 %triangle_updates.1 = bf16[128,8,128]{2,1,0:T(8,128)(2,1)S(1)} custom-call(s32[1,128]{1,0:T(1,128)S(1)} %bitcast.5, bf16[8,128,128]{2,1,0:T(8,128)(2,1)S(1)} %copy-done, bf16[2,128,512]{2,1,0:T(8,128)(2,1)S(1)} %copy-done.1, bf16[2,128,128]{2,1,0:T(8,128)(2,1)S(1)} %copy-done.2, bf16[2,128,128]{2,1,0:T(8,128)(2,1)S(1)} %copy-done.3, f32[4,128]{1,0:T(4,128)S(1)} %bitcast.4), custom_call_target="tpu_custom_call" | custom-call | tf_op jit(solution)/shard_map/triangle_updates/pallas_call | solution.py:378
  54.0 0.9 %copy.7 = bf16[8,128,128]{2,1,0:T(8,128)(2,1)} copy(bf16[8,128,128]{1,0,2:T(8,128)(2,1)S(1)} %bitcast.3) | data formatting | bytes 524288 | tf_op jit(solution)/shard_map/transpose | solution.py:405
Async XLA Ops:
  0.0 0.7 %copy-start.4 = (f32[2,2,128]{2,1,0:T(2,128)S(1)}, f32[2,2,128]{2,1,0:T(2,128)}, u32[]{:S(2)}) copy-start(f32[2,2,128]{2,1,0:T(2,128)} %param.11) | copy-start | bytes 6148
  0.0 0.7 %copy-start.5 = (s32[128]{0:T(128)S(1)}, s32[128]{0:T(128)}, u32[]{:S(2)}) copy-start(s32[128]{0:T(128)} %param.7) | copy-start | bytes 1540
  0.7 1.0 %copy-start = (bf16[8,128,128]{2,1,0:T(8,128)(2,1)S(1)}, bf16[8,128,128]{2,1,0:T(8,128)(2,1)}, u32[]{:S(2)}) copy-start(bf16[8,128,128]{2,1,0:T(8,128)(2,1)} %pair_h.1) | copy-start | bytes 786436
  1.6 0.9 %copy-start.1 = (bf16[2,128,512]{2,1,0:T(8,128)(2,1)S(1)}, bf16[2,128,512]{2,1,0:T(8,128)(2,1)}, u32[]{:S(2)}) copy-start(bf16[2,128,512]{2,1,0:T(8,128)(2,1)} %proj_h.1) | copy-start | bytes 786436
  2.6 0.8 %copy-start.2 = (bf16[2,128,128]{2,1,0:T(8,128)(2,1)S(1)}, bf16[2,128,128]{2,1,0:T(8,128)(2,1)}, u32[]{:S(2)}) copy-start(bf16[2,128,128]{2,1,0:T(8,128)(2,1)} %gate_h.1) | copy-start | bytes 196612
  3.4 0.8 %copy-start.3 = (bf16[2,128,128]{2,1,0:T(8,128)(2,1)S(1)}, bf16[2,128,128]{2,1,0:T(8,128)(2,1)}, u32[]{:S(2)}) copy-start(bf16[2,128,128]{2,1,0:T(8,128)(2,1)} %out_h.1) | copy-start | bytes 196612

commit v3 on v2

--- a/solution.py
+++ b/solution.py
@@ -97,7 +97,7 @@
     out,
     mask_v, pair, proj, gate_w, out_w, gains,
     state, normed, gates,
-    right_f, left_f, right_b, prod0, edge_f, prod1,
+    right_f, left_f, prod0, edge_f, prod1,
     right_send, right_recv, left_send, left_recv, back_send, back_recv,
     edge_send, edge_recv, done_send, done_recv,
     load_sem, send_sem, recv_sem,
@@ -106,7 +106,7 @@
     chan = pair.shape[2]
     res = pair.shape[1]
     half = ring // 2
-    group = chan // half
+    cuts = chan // half // SUBL
     place = lax.rem(me, half)
     base = me - place
     per = rows // CHUNKS
@@ -147,7 +147,7 @@
     def slot(device):
         return lax.rem(device, half)
 
-    span = per * group
+    span = per * SUBL
 
     def part(ch):
         return pl.ds(ch * span, span)
@@ -190,25 +190,37 @@
             if side == 1 and ch > 0:
                 norm_rows(ch, gains_t[:, 0:1])
             block = masked(ch, edges(ch, proj_t[2 * side * chan : 2 * (side + 1) * chan]))
-            for k in range(per):
-                at = (ch * per + k) * group
-                buf[:, at : at + group, :] = block[k].reshape(half, group, res).astype(BF16)
+            for d in range(duos):
+                two = [block[2 * d + k].reshape(half, cuts, SUBL, res) for k in (0, 1)]
+                at = ch * span + d * 16
+                for cut in range(cuts):
+                    buf[cut, :, at : at + 16, :] = jnp.concatenate(
+                        [x[:, cut] for x in two], axis=1
+                    ).astype(BF16)
             if side == 1:
                 if ch == 0:
                     pl.semaphore_wait(barrier, ring - 1)
                 for o in everyone:
                     to = far(o)
                     copy(
-                        right_send.at[slot(to), part(ch)], right_recv.at[me, part(ch)],
+                        right_send.at[0, slot(to), part(ch)], right_recv.at[0, me, part(ch)],
                         to, RIGHT, ch, me,
                     ).start()
-            else:
+        if side == 0:
+            for cut in range(cuts):
                 for o in nearby:
                     to = near(o)
                     copy(
-                        left_send.at[slot(to), part(ch)], left_recv.at[place, part(ch)],
-                        to, LEFT, ch, me,
+                        left_send.at[cut, slot(to)], left_recv.at[cut, place],
+                        to, LEFT, cut, me,
                     ).start()
+                if cut + 1 < cuts:
+                    for o in everyone:
+                        to = far(o)
+                        copy(
+                            right_send.at[cut + 1, slot(to)], right_recv.at[cut + 1, me],
+                            to, RIGHT, CHUNKS + cut, me,
+                        ).start()
 
     loads[4].wait()
     loads[5].wait()
@@ -217,65 +229,75 @@
     for ch in range(CHUNKS):
         gates[ch] = sigmoid(jnp.dot(gate_t[0], normed[ch], preferred_element_type=F32))
 
-    def hold_right(device, ch, values):
-        at = pl.multiple_of(device * (rows * group) + ch * span, span)
-        right_f[pl.ds(at, span), :] = values.astype(F32)
-
-    def hold_left(where, ch, values):
-        at = pl.multiple_of(ch * (half * span) + where * span, span)
-        left_f[pl.ds(at, span), :] = values.astype(F32)
-
-    for ch in range(CHUNKS):
-        hold_right(me, ch, right_send[place, part(ch), :])
-        hold_left(place, ch, left_send[place, part(ch), :])
-    for ch in range(CHUNKS):
+    block_rows = rows * SUBL
+    count = half * rows
+    for cut in range(cuts):
+        at = pl.multiple_of(me * block_rows, block_rows)
+        right_f[cut, pl.ds(at, block_rows), :] = right_send[cut, place].astype(F32)
+        at = pl.multiple_of(place * block_rows, block_rows)
+        left_f[cut, pl.ds(at, block_rows), :] = left_send[cut, place].astype(F32)
+
+    def give(cut, where, ch):
+        for d in range(ch * duos, (ch + 1) * duos):
+            parts = [
+                prod0.at[cut][pl.ds(where * rows + 2 * d + k, SUBL, stride=count), :]
+                for k in (0, 1)
+            ]
+            back_send[cut, where, d * 16 : (d + 1) * 16, :] = jnp.concatenate(
+                parts, axis=0
+            ).astype(BF16)
+
+    for cut in range(cuts):
         for o in reversed(everyone):
             frm = far(o)
-            landed = right_recv.at[frm, part(ch)]
-            copy(landed, landed, frm, RIGHT, ch, frm).wait_recv()
-            hold_right(frm, ch, right_recv[frm, part(ch), :])
-    for c in range(group):
-        right_b[c] = right_f[pl.ds(c, res, stride=group), :].astype(BF16)
-    count = half * per
-    for ch in range(CHUNKS):
+            if cut == 0:
+                for ch in range(CHUNKS):
+                    landed = right_recv.at[0, frm, part(ch)]
+                    copy(landed, landed, frm, RIGHT, ch, frm).wait_recv()
+            else:
+                landed = right_recv.at[cut, frm]
+                copy(landed, landed, frm, RIGHT, CHUNKS + cut - 1, frm).wait_recv()
+            at = pl.multiple_of(frm * block_rows, block_rows)
+            right_f[cut, pl.ds(at, block_rows), :] = right_recv[cut, frm].astype(F32)
         for o in reversed(nearby):
             frm = near(o)
-            landed = left_recv.at[slot(frm), part(ch)]
-            copy(landed, landed, frm, LEFT, ch, frm).wait_recv()
-            hold_left(slot(frm), ch, left_recv[slot(frm), part(ch), :])
-        for c in range(group):
-            left = left_f[pl.ds(ch * half * span + c, count, stride=group), :].astype(BF16)
-            prod0[ch, c * count : (c + 1) * count, :] = lax.dot_general(
-                left, right_b[c], (((1,), (1,)), ((), ())), preferred_element_type=F32
+            landed = left_recv.at[cut, slot(frm)]
+            copy(landed, landed, frm, LEFT, cut, frm).wait_recv()
+            at = pl.multiple_of(slot(frm) * block_rows, block_rows)
+            left_f[cut, pl.ds(at, block_rows), :] = left_recv[cut, slot(frm)].astype(F32)
+        for c in range(SUBL):
+            left = left_f.at[cut][pl.ds(c, count, stride=SUBL), :].astype(BF16)
+            right = right_f.at[cut][pl.ds(c, res, stride=SUBL), :].astype(BF16)
+            prod0[cut, c * count : (c + 1) * count, :] = lax.dot_general(
+                left, right, (((1,), (1,)), ((), ())), preferred_element_type=F32
             )
-
-        def give(where):
-            for k in range(per):
-                at = (ch * per + k) * group
-                rows_of = prod0.at[ch][pl.ds(where * per + k, group, stride=count), :]
-                back_send[where, at : at + group, :] = rows_of.astype(BF16)
-
-        for o in nearby:
-            to = near(o)
-            give(slot(to))
-            copy(
-                back_send.at[slot(to), part(ch)], back_recv.at[place, part(ch)],
-                to, BACK, ch, me,
-            ).start()
-        give(place)
-        back_recv[place, part(ch), :] = back_send[place, part(ch), :]
+        for ch in range(CHUNKS):
+            for o in nearby:
+                to = near(o)
+                give(cut, slot(to), ch)
+                copy(
+                    back_send.at[cut, slot(to), part(ch)], back_recv.at[cut, place, part(ch)],
+                    to, BACK, cut * CHUNKS + ch, me,
+                ).start()
+            give(cut, place, ch)
+            back_recv[cut, place, part(ch), :] = back_send[cut, place, part(ch), :]
 
     proj_t = proj[1].astype(F32).T.astype(BF16)
     size = per * SUBL
     for ch in range(CHUNKS):
         for o in reversed(nearby):
             frm = near(o)
-            landed = back_recv.at[slot(frm), part(ch)]
-            copy(landed, landed, frm, BACK, ch, frm).wait_recv()
+            for cut in range(cuts):
+                landed = back_recv.at[cut, slot(frm), part(ch)]
+                copy(landed, landed, frm, BACK, cut * CHUNKS + ch, frm).wait_recv()
         for k in range(per):
             r = ch * per + k
-            got = back_recv[:, r * group : (r + 1) * group, :].reshape(chan, res)
-            pn = norm_lead(got.astype(F32), gains_t[:, 1:2]).astype(BF16)
+            tile = slice((r // 2) * 16, (r // 2 + 1) * 16)
+            mine = slice((r % 2) * SUBL, (r % 2 + 1) * SUBL)
+            got = jnp.stack(
+                [back_recv[cut, :, tile, :].astype(F32)[:, mine] for cut in range(cuts)], axis=1
+            ).reshape(chan, res)
+            pn = norm_lead(got, gains_t[:, 1:2]).astype(BF16)
             update = jnp.dot(out_t[0], pn, preferred_element_type=F32)
             new = state[r] + gates[ch, :, k * res : (k + 1) * res] * update
             state[r] = new.astype(BF16).astype(F32)
@@ -344,32 +366,34 @@
                 new = state[r] + gates[ch, :, k * res : (k + 1) * res] * update
                 out[:, r, :] = new.astype(BF16)
 
-    for ch in range(CHUNKS):
-        for o in everyone:
-            to = far(o)
-            for kind, src in (
-                (RIGHT, right_send.at[slot(to), part(ch)]),
-                (EDGE, edge_send.at[ch, to]),
-                (DONE, done_send.at[ch, to]),
-            ):
-                copy(src, src, to, kind, ch, to).wait_send()
-        for o in nearby:
-            to = near(o)
-            for kind, src in (
-                (LEFT, left_send.at[slot(to), part(ch)]),
-                (BACK, back_send.at[slot(to), part(ch)]),
-            ):
-                copy(src, src, to, kind, ch, to).wait_send()
+    for o in everyone:
+        to = far(o)
+        sent = [(RIGHT, ch, right_send.at[0, slot(to), part(ch)]) for ch in range(CHUNKS)]
+        sent += [
+            (RIGHT, CHUNKS + cut - 1, right_send.at[cut, slot(to)]) for cut in range(1, cuts)
+        ]
+        sent += [(EDGE, ch, edge_send.at[ch, to]) for ch in range(CHUNKS)]
+        sent += [(DONE, ch, done_send.at[ch, to]) for ch in range(CHUNKS)]
+        for kind, at, src in sent:
+            copy(src, src, to, kind, at, to).wait_send()
+    for o in nearby:
+        to = near(o)
+        for cut in range(cuts):
+            src = left_send.at[cut, slot(to)]
+            copy(src, src, to, LEFT, cut, to).wait_send()
+            for ch in range(CHUNKS):
+                src = back_send.at[cut, slot(to), part(ch)]
+                copy(src, src, to, BACK, cut * CHUNKS + ch, to).wait_send()
 
 
 def fused(ring, pair, residue_mask, tri_proj, gate_out, w_out, norm_gain):
     rows, res, chan = pair.shape
     half = ring // 2
-    group = chan // half
+    cuts = chan // half // SUBL
     per = rows // CHUNKS
     wide = (CHUNKS, chan, per * res)
-    right_all = pltpu.VMEM((ring, rows * group, res), BF16)
-    near_all = pltpu.VMEM((half, rows * group, res), BF16)
+    right_all = pltpu.VMEM((cuts, ring, rows * SUBL, res), BF16)
+    near_all = pltpu.VMEM((cuts, half, rows * SUBL, res), BF16)
     edge_all = pltpu.VMEM((CHUNKS, ring, 2 * per * SUBL, res), BF16)
     done_all = pltpu.VMEM((CHUNKS, ring, per * SUBL, res), BF16)
     operands = (
@@ -378,27 +402,26 @@
     out = pl.pallas_call(
         functools.partial(kernel, ring, rows),
         out_shape=jax.ShapeDtypeStruct((chan, rows, res), BF16),
-        in_specs=[pl.BlockSpec(memory_space=pl.ANY)] * 6,
+        in_specs=[pl.BlockSpec(memory_space=pltpu.HBM)] * 6,
         out_specs=pl.BlockSpec(memory_space=pltpu.VMEM),
         scratch_shapes=[pltpu.VMEM(x.shape, x.dtype) for x in operands]
         + [
             pltpu.VMEM((rows, chan, res), F32),
             pltpu.VMEM(wide, BF16),
             pltpu.VMEM(wide, F32),
-            pltpu.VMEM((ring * rows * group, res), F32),
-            pltpu.VMEM((half * rows * group, res), F32),
-            pltpu.VMEM((group, res, res), BF16),
-            pltpu.VMEM((CHUNKS, group * half * per, res), F32),
+            pltpu.VMEM((cuts, ring * rows * SUBL, res), F32),
+            pltpu.VMEM((cuts, half * rows * SUBL, res), F32),
+            pltpu.VMEM((cuts, SUBL * half * rows, res), F32),
             pltpu.VMEM((2, ring * rows * SUBL, res), F32),
             pltpu.VMEM((SUBL * res, res), F32),
             near_all, right_all, near_all, near_all, near_all, near_all,
             edge_all, edge_all, done_all, done_all,
             pltpu.SemaphoreType.DMA((6,)),
-            pltpu.SemaphoreType.DMA((5, CHUNKS, ring)),
-            pltpu.SemaphoreType.DMA((5, CHUNKS, ring)),
+            pltpu.SemaphoreType.DMA((5, cuts * CHUNKS, ring)),
+            pltpu.SemaphoreType.DMA((5, cuts * CHUNKS, ring)),
         ],
         compiler_params=pltpu.CompilerParams(
-            collective_id=0, has_side_effects=True, vmem_limit_bytes=40 * 1024 * 1024
+            collective_id=0, has_side_effects=True, vmem_limit_bytes=62 * 1024 * 1024
         ),
         name="triangle_updates",
     )(*operands)

time: 55.1 us -> 55 us (level)
  local copies, waits for them, and re-layouts: 5.16 us -> 1.82 us
  Pallas kernels: 49.7 us -> 53 us
    unnamed x12 -> x0, local copies, waits for them, and re-layouts: 4.26 us -> none
    pallas_call x1, Pallas kernels: 49.7 us -> 53 us  [fused(): pl.pallas_call(functools.partial(kernel, ring, rows), out_shape=jax.Shape...]
    transpose x1, local copies, waits for them, and re-layouts: 0.9 us -> 1.82 us  [fused(): return jnp.moveaxis(out, 0, 2)]
where the time goes in v3:
time: 55 us; the launch traced here: 54.8 us
  Pallas kernels  53 us (96%)
  local copies, waits for them, and re-layouts  1.82 us (3%)
    pallas_call x1, Pallas kernels, fused(): pl.pallas_call(functools.partial(kernel, ring, rows), out_shape=jax.Shape...  53 us
    transpose x1, local copies, waits for them, and re-layouts, fused(): return jnp.moveaxis(out, 0, 2)  1.82 us

profile of v3, /device:TPU:0, one launch (start us, length us, event | category | flops | bytes accessed | tf_op | source)
XLA Modules:
  0.0 54.8 jit_solution(4519179633704395696)
XLA Ops:
  0.0 53.0 %triangle_updates.1 = bf16[128,8,128]{2,1,0:T(8,128)(2,1)} custom-call(s32[1,128]{1,0:T(1,128)} %bitcast.5, bf16[8,128,128]{2,1,0:T(8,128)(2,1)} %pair_h.1, bf16[2,128,512]{2,1,0:T(8,128)(2,1)} %proj_h.1, bf16[2,128,128]{2,1,0:T(8,128)(2,1)} %gate_h.1, bf16[2,128,128]{2,1,0:T(8,128)(2,1)} %out_h.1, f32[4,128]{1,0:T(4,128)} %bitcast.4), custom_call_target="tpu_custom_call" | custom-call | tf_op jit(solution)/shard_map/triangle_updates/pallas_call | solution.py:402
  53.0 1.8 %copy.7 = bf16[8,128,128]{2,1,0:T(8,128)(2,1)} copy(bf16[8,128,128]{1,0,2:T(8,128)(2,1)} %bitcast.3) | data formatting | bytes 524288 | tf_op jit(solution)/shard_map/transpose | solution.py:428

commit v4 on v3

--- a/solution.py
+++ b/solution.py
@@ -131,12 +131,20 @@
             device_id_type=pl.DeviceIdType.MESH,
         )
 
-    def copy(src, dst, to, kind, ch, frm):
+    def copy(src, dst, to, kind, ch):
         return pltpu.make_async_remote_copy(
             src_ref=src, dst_ref=dst,
-            send_sem=send_sem.at[kind, ch, to], recv_sem=recv_sem.at[kind, ch, frm],
+            send_sem=send_sem.at[kind, ch], recv_sem=recv_sem.at[kind, ch],
             device_id={"row": to}, device_id_type=pl.DeviceIdType.MESH,
         )
+
+    def arrived(blocks, kind, ch):
+        copy(blocks, blocks, far(1), kind, ch).wait_recv()
+
+    def left_here(blocks, kind, ch):
+        copy(blocks, blocks, far(1), kind, ch).wait_send()
+
+    others, neighbours = pl.ds(0, ring - 1), pl.ds(0, half - 1)
 
     def far(o):
         return lax.rem(me + o, ring)
@@ -204,7 +212,7 @@
                     to = far(o)
                     copy(
                         right_send.at[0, slot(to), part(ch)], right_recv.at[0, me, part(ch)],
-                        to, RIGHT, ch, me,
+                        to, RIGHT, ch,
                     ).start()
         if side == 0:
             for cut in range(cuts):
@@ -212,14 +220,14 @@
                     to = near(o)
                     copy(
                         left_send.at[cut, slot(to)], left_recv.at[cut, place],
-                        to, LEFT, cut, me,
+                        to, LEFT, cut,
                     ).start()
                 if cut + 1 < cuts:
                     for o in everyone:
                         to = far(o)
                         copy(
                             right_send.at[cut + 1, slot(to)], right_recv.at[cut + 1, me],
-                            to, RIGHT, CHUNKS + cut, me,
+                            to, RIGHT, CHUNKS + cut,
                         ).start()
 
     loads[4].wait()
@@ -248,21 +256,18 @@
             ).astype(BF16)
 
     for cut in range(cuts):
+        if cut == 0:
+            for ch in range(CHUNKS):
+                arrived(right_recv.at[0, others, part(ch)], RIGHT, ch)
+        else:
+            arrived(right_recv.at[cut, others], RIGHT, CHUNKS + cut - 1)
         for o in reversed(everyone):
             frm = far(o)
-            if cut == 0:
-                for ch in range(CHUNKS):
-                    landed = right_recv.at[0, frm, part(ch)]
-                    copy(landed, landed, frm, RIGHT, ch, frm).wait_recv()
-            else:
-                landed = right_recv.at[cut, frm]
-                copy(landed, landed, frm, RIGHT, CHUNKS + cut - 1, frm).wait_recv()
             at = pl.multiple_of(frm * block_rows, block_rows)
             right_f[cut, pl.ds(at, block_rows), :] = right_recv[cut, frm].astype(F32)
+        arrived(left_recv.at[cut, neighbours], LEFT, cut)
         for o in reversed(nearby):
             frm = near(o)
-            landed = left_recv.at[cut, slot(frm)]
-            copy(landed, landed, frm, LEFT, cut, frm).wait_recv()
             at = pl.multiple_of(slot(frm) * block_rows, block_rows)
             left_f[cut, pl.ds(at, block_rows), :] = left_recv[cut, slot(frm)].astype(F32)
         for c in range(SUBL):
@@ -277,7 +282,7 @@
                 give(cut, slot(to), ch)
                 copy(
                     back_send.at[cut, slot(to), part(ch)], back_recv.at[cut, place, part(ch)],
-                    to, BACK, cut * CHUNKS + ch, me,
+                    to, BACK, cut * CHUNKS + ch,
                 ).start()
             give(cut, place, ch)
             back_recv[cut, place, part(ch), :] = back_send[cut, place, part(ch), :]
@@ -285,11 +290,8 @@
     proj_t = proj[1].astype(F32).T.astype(BF16)
     size = per * SUBL
     for ch in range(CHUNKS):
-        for o in reversed(nearby):
-            frm = near(o)
-            for cut in range(cuts):
-                landed = back_recv.at[cut, slot(frm), part(ch)]
-                copy(landed, landed, frm, BACK, cut * CHUNKS + ch, frm).wait_recv()
+        for cut in range(cuts):
+            arrived(back_recv.at[cut, neighbours, part(ch)], BACK, cut * CHUNKS + ch)
         for k in range(per):
             r = ch * per + k
             tile = slice((r // 2) * 16, (r // 2 + 1) * 16)
@@ -312,7 +314,7 @@
                 ).astype(BF16)
         for o in everyone:
             to = far(o)
-            copy(edge_send.at[ch, to], edge_recv.at[ch, me], to, EDGE, ch, me).start()
+            copy(edge_send.at[ch, to], edge_recv.at[ch, me], to, EDGE, ch).start()
 
     for ch in range(CHUNKS):
         gates[ch] = sigmoid(jnp.dot(gate_t[1], normed[ch], preferred_element_type=F32))
@@ -324,10 +326,9 @@
 
     for ch in range(CHUNKS):
         hold_edges(me, ch, edge_send[ch, me])
+        arrived(edge_recv.at[ch, others], EDGE, ch)
         for o in reversed(everyone):
             frm = far(o)
-            landed = edge_recv.at[ch, frm]
-            copy(landed, landed, frm, EDGE, ch, frm).wait_recv()
             hold_edges(frm, ch, edge_recv[ch, frm])
     for c in range(SUBL):
         left = edge_f.at[0][pl.ds(c, res, stride=SUBL), :].T.astype(BF16)
@@ -346,15 +347,12 @@
         for o in everyone:
             to = far(o)
             give_back(to)
-            copy(done_send.at[ch, to], done_recv.at[ch, me], to, DONE, ch, me).start()
+            copy(done_send.at[ch, to], done_recv.at[ch, me], to, DONE, ch).start()
         give_back(me)
         done_recv[ch, me] = done_send[ch, me]
 
     for ch in range(CHUNKS):
-        for o in reversed(everyone):
-            frm = far(o)
-            landed = done_recv.at[ch, frm]
-            copy(landed, landed, frm, DONE, ch, frm).wait_recv()
+        arrived(done_recv.at[ch, others], DONE, ch)
         for d in range(duos):
             got = done_recv[ch, :, d * 16 : (d + 1) * 16, :].astype(F32)
             for j in (0, 1):
@@ -366,24 +364,16 @@
                 new = state[r] + gates[ch, :, k * res : (k + 1) * res] * update
                 out[:, r, :] = new.astype(BF16)
 
-    for o in everyone:
-        to = far(o)
-        sent = [(RIGHT, ch, right_send.at[0, slot(to), part(ch)]) for ch in range(CHUNKS)]
-        sent += [
-            (RIGHT, CHUNKS + cut - 1, right_send.at[cut, slot(to)]) for cut in range(1, cuts)
-        ]
-        sent += [(EDGE, ch, edge_send.at[ch, to]) for ch in range(CHUNKS)]
-        sent += [(DONE, ch, done_send.at[ch, to]) for ch in range(CHUNKS)]
-        for kind, at, src in sent:
-            copy(src, src, to, kind, at, to).wait_send()
-    for o in nearby:
-        to = near(o)
-        for cut in range(cuts):
-            src = left_send.at[cut, slot(to)]
-            copy(src, src, to, LEFT, cut, to).wait_send()
-            for ch in range(CHUNKS):
-                src = back_send.at[cut, slot(to), part(ch)]
-                copy(src, src, to, BACK, cut * CHUNKS + ch, to).wait_send()
+    for ch in range(CHUNKS):
+        left_here(right_recv.at[0, others, part(ch)], RIGHT, ch)
+        left_here(edge_recv.at[ch, others], EDGE, ch)
+        left_here(done_recv.at[ch, others], DONE, ch)
+    for cut in range(cuts):
+        if cut > 0:
+            left_here(right_recv.at[cut, others], RIGHT, CHUNKS + cut - 1)
+        left_here(left_recv.at[cut, neighbours], LEFT, cut)
+        for ch in range(CHUNKS):
+            left_here(back_recv.at[cut, neighbours, part(ch)], BACK, cut * CHUNKS + ch)
 
 
 def fused(ring, pair, residue_mask, tri_proj, gate_out, w_out, norm_gain):
@@ -417,8 +407,8 @@
             near_all, right_all, near_all, near_all, near_all, near_all,
             edge_all, edge_all, done_all, done_all,
             pltpu.SemaphoreType.DMA((6,)),
-            pltpu.SemaphoreType.DMA((5, cuts * CHUNKS, ring)),
-            pltpu.SemaphoreType.DMA((5, cuts * CHUNKS, ring)),
+            pltpu.SemaphoreType.DMA((5, cuts * CHUNKS)),
+            pltpu.SemaphoreType.DMA((5, cuts * CHUNKS)),
         ],
         compiler_params=pltpu.CompilerParams(
             collective_id=0, has_side_effects=True, vmem_limit_bytes=62 * 1024 * 1024

time: 55 us -> 49.4 us (0.90)
  Pallas kernels: 53 us -> 47.4 us
    pallas_call x1, Pallas kernels: 53 us -> 47.4 us  [fused(): pl.pallas_call(functools.partial(kernel, ring, rows), out_shape=jax.Shape...]
where the time goes in v4:
time: 49.4 us; the launch traced here: 49.3 us
  Pallas kernels  47.4 us (96%)
  local copies, waits for them, and re-layouts  1.82 us (4%)
    pallas_call x1, Pallas kernels, fused(): pl.pallas_call(functools.partial(kernel, ring, rows), out_shape=jax.Shape...  47.4 us
    transpose x1, local copies, waits for them, and re-layouts, fused(): return jnp.moveaxis(out, 0, 2)  1.82 us

profile of v4, /device:TPU:0, one launch (start us, length us, event | category | flops | bytes accessed | tf_op | source)
XLA Modules:
  0.0 49.3 jit_solution(5690724640804454834)
XLA Ops:
  0.0 47.4 %triangle_updates.1 = bf16[128,8,128]{2,1,0:T(8,128)(2,1)} custom-call(s32[1,128]{1,0:T(1,128)} %bitcast.5, bf16[8,128,128]{2,1,0:T(8,128)(2,1)} %pair_h.1, bf16[2,128,512]{2,1,0:T(8,128)(2,1)} %proj_h.1, bf16[2,128,128]{2,1,0:T(8,128)(2,1)} %gate_h.1, bf16[2,128,128]{2,1,0:T(8,128)(2,1)} %out_h.1, f32[4,128]{1,0:T(4,128)} %bitcast.4), custom_call_target="tpu_custom_call" | custom-call | tf_op jit(solution)/shard_map/triangle_updates/pallas_call | solution.py:392
  47.4 1.8 %copy.7 = bf16[8,128,128]{2,1,0:T(8,128)(2,1)} copy(bf16[8,128,128]{1,0,2:T(8,128)(2,1)} %bitcast.3) | data formatting | bytes 524288 | tf_op jit(solution)/shard_map/transpose | solution.py:418

commit v5 on v4

--- a/solution.py
+++ b/solution.py
@@ -362,7 +362,7 @@
                 pn = norm_lead(block, gains_t[:, 3:4]).astype(BF16)
                 update = jnp.dot(out_t[1], pn, preferred_element_type=F32)
                 new = state[r] + gates[ch, :, k * res : (k + 1) * res] * update
-                out[:, r, :] = new.astype(BF16)
+                out[r] = new.T.astype(BF16)
 
     for ch in range(CHUNKS):
         left_here(right_recv.at[0, others, part(ch)], RIGHT, ch)
@@ -389,9 +389,9 @@
     operands = (
         residue_mask.reshape(1, res), pair, tri_proj, gate_out, w_out, norm_gain.reshape(4, chan),
     )
-    out = pl.pallas_call(
+    return pl.pallas_call(
         functools.partial(kernel, ring, rows),
-        out_shape=jax.ShapeDtypeStruct((chan, rows, res), BF16),
+        out_shape=jax.ShapeDtypeStruct((rows, res, chan), BF16),
         in_specs=[pl.BlockSpec(memory_space=pltpu.HBM)] * 6,
         out_specs=pl.BlockSpec(memory_space=pltpu.VMEM),
         scratch_shapes=[pltpu.VMEM(x.shape, x.dtype) for x in operands]
@@ -415,7 +415,6 @@
         ),
         name="triangle_updates",
     )(*operands)
-    return jnp.moveaxis(out, 0, 2)
 
 
 def on_device(ring, pair, *rest):

time: 49.4 us -> 49.1 us (level)
    transpose x1 -> x0, local copies, waits for them, and re-layouts: 1.82 us -> none  [fused(): return jnp.moveaxis(out, 0, 2)]
    unnamed x0 -> x1, local copies, waits for them, and re-layouts: none -> 1.67 us
where the time goes in v5:
time: 49.1 us; the launch traced here: 48.9 us
  Pallas kernels  47.2 us (96%)
  local copies, waits for them, and re-layouts  1.67 us (3%)
    pallas_call x1, Pallas kernels, fused(): pl.pallas_call(functools.partial(kernel, ring, rows), out_shape=jax.Shape...  47.2 us
    unnamed x1, local copies, waits for them, and re-layouts  1.67 us

profile of v5, /device:TPU:0, one launch (start us, length us, event | category | flops | bytes accessed | tf_op | source)
XLA Modules:
  0.0 48.9 jit_solution(5772902230101083676)
XLA Ops:
  0.0 47.2 %triangle_updates.1 = bf16[8,128,128]{2,1,0:T(8,128)(2,1)} custom-call(s32[1,128]{1,0:T(1,128)} %bitcast.3, bf16[8,128,128]{2,1,0:T(8,128)(2,1)} %pair_h.1, bf16[2,128,512]{2,1,0:T(8,128)(2,1)} %proj_h.1, bf16[2,128,128]{2,1,0:T(8,128)(2,1)} %gate_h.1, bf16[2,128,128]{2,1,0:T(8,128)(2,1)} %out_h.1, f32[4,128]{1,0:T(4,128)} %bitcast.2), custom_call_target="tpu_custom_call" | custom-call | tf_op jit(solution)/shard_map/triangle_updates/pallas_call | solution.py:392
  47.2 1.7 %copy.8 = bf16[8,128,128]{2,1,0:T(8,128)(2,1)} copy(bf16[8,128,128]{2,1,0:T(8,128)(2,1)} %triangle_updates.1) | data formatting | bytes 524288
